TPU v7x, 256 devices: a whole 4x4x8 slice. The times are simulated.
256 devices in a mesh: layer: 16 (over y_lo, x, core), query: 16 (over z, y_hi).
Axes of the slice: x: 4, y: 4 (y_hi: 2, y_lo: 2; y = y_hi * 2 + y_lo), z: 8, core: 2. Of those that a mesh axis runs over, the one named last changes fastest.
Arguments:
- queries: bfloat16 [16384, 16, 4096], P('query', 'layer'), may hold values from -6 to 6
- train_grads: bfloat16 [1024, 16, 4096], P('query', 'layer'), may hold values from -6 to 6
- basis_out: float32 [16, 64, 64], P('layer'), may hold values from -0.75 to 0.75
- basis_in: float32 [16, 64, 64], P('layer'), may hold values from -0.75 to 0.75
- eig_values: float32 [16, 4096], P('layer'), may hold values from 0.1 to 2
- train_order: int32 [1024], replicated, may hold values from 0 to 1023, each once
Outputs:
- scores: float32 [1024, 16384], P('layer', 'query')
Inputs may be any that keep to these rules, and one draw needn't show every extreme that they name: `train_order`: a permutation of the 1024 training examples.
All inputs are finite; a program needn't handle non-finite values.
Results may differ from a plain program's by a relative error of at most 0.0029.
Values may be sent and summed in bfloat16 or wider, within the bound.
No kernel may reach another device: no remote copies, remote signals or barrier semaphores. Data moves between devices by JAX's collectives and lax.ppermute only.
A program may use at most 64 MiB of HBM per device.

v0:
```python
import jax
import jax.numpy as jnp
from jax import lax
from jax.sharding import PartitionSpec as P


def per_device(queries, train_grads, basis_out, basis_in, eig_values, train_order):
    query_rows, local_layers, feat_size = queries.shape
    train_rows = train_grads.shape[0]
    side = basis_out.shape[1]
    grads_full = train_grads.astype(jnp.float32).reshape(train_rows, local_layers, side, side)
    rotated = jnp.einsum(
        "lab,elac,lcd->elbd", basis_out, grads_full, basis_in, precision=lax.Precision.HIGHEST
    )
    scaled = (rotated.reshape(train_rows, local_layers, feat_size) / eig_values[None]).astype(
        jnp.bfloat16
    )
    scaled_flat = scaled.reshape(train_rows, local_layers * feat_size)
    query_flat = queries.reshape(query_rows, local_layers * feat_size)
    layer_devices = lax.axis_size("layer")
    factor = 1.0 / jnp.sqrt(jnp.float32(local_layers * layer_devices * feat_size))
    partial_sum = lax.dot_general(
        lax.all_gather(scaled_flat, "query", axis=0, tiled=True),
        query_flat,
        (((1,), (1,)), ((), ())),
        preferred_element_type=jnp.float32,
    )
    ordered = partial_sum[train_order] * factor
    return lax.psum_scatter(ordered, "layer", scatter_dimension=0, tiled=True)


def solution(mesh):
    placed = (
        P("query", "layer", None),
        P("query", "layer", None),
        P("layer", None, None),
        P("layer", None, None),
        P("layer", None),
        P(),
    )
    return jax.shard_map(
        per_device, mesh=mesh, in_specs=placed, out_specs=P("layer", "query"), check_vma=False
    )
```

profile of v0, /device:TPU:16, one launch (start us, length us, event | category | flops | bytes accessed | tf_op | source)
XLA Modules:
  0.0 253.4 jit_solution(12795032566997530325)
XLA Ops:
  6.5 0.0 copy-start
  6.5 0.0 copy-start.1
  6.5 0.0 all-gather.2.cloned.1.call-start
  6.5 2.1 reshape.35
  8.6 0.0 copy-done
  8.6 1.0 fusion.4
  9.7 0.0 copy-done.1
  9.7 0.0 copy-start.2
  9.7 0.0 copy-start.3
  9.7 1.8 fusion.2
  11.6 0.7 transpose.5
  12.2 0.0 copy-done.2
  12.2 0.9 divide_convert_fusion
  13.1 0.0 all-gather.2.cloned.1.call-update
  13.2 0.0 reduce-scatter.2.cloned.1.call-start
  13.2 0.0 copy-done.3
  13.2 136.2 %all-gather.2.cloned.1.call-done = bf16[1024,4096]{1,0:T(8,128)(2,1)} async-done(((bf16[64,4096]{1,0:T(8,128)(2,1)}), bf16[1024,4096]{1,0:T(8,128)(2,1)}) %all-gather.2.cloned.1.call-update) | async-done | bytes 8388624 | tf_op jit(solution)/shard_map/all_gather | solution.py:23
  149.4 15.1 %fusion = f32[1024,1024]{1,0:T(8,128)} fusion(bf16[1024,4096]{1,0:T(8,128)(2,1)} %all-gather.2.cloned.1.call-done, bf16[1024,1,4096]{2,0,1:T(8,128)(2,1)} %param.6), kind=kOutput, calls=%fused_computation.1 | convolution fusion | flops 8589934592 | bytes 20971520 | tf_op jit(solution)/shard_map/dot_general | solution.py:22
  164.5 8.5 %gather_fusion = f32[1024,1024]{1,0:T(8,128)} fusion(f32[1024,1024]{1,0:T(8,128)} %fusion, s32[1024]{0:T(1024)S(1)} %fusion.6), kind=kCustom, calls=%fused_computation | custom fusion | bytes 8392704 | tf_op jit(solution)/shard_map/gather | solution.py:28
  173.1 5.0 %broadcast_multiply_fusion = f32[1024,1024]{1,0:T(8,128)} fusion(f32[1024,1024]{1,0:T(8,128)} %gather_fusion), kind=kLoop, calls=%fused_computation.3 | loop fusion | flops 1048576 | bytes 8388608 | tf_op jit(solution)/shard_map/mul | solution.py:28
  178.0 0.0 reduce-scatter.2.cloned.1.call-update
  178.0 68.5 %reduce-scatter.2.cloned.1.call-done = f32[64,1024]{1,0:T(8,128)} async-done(((f32[1024,1024]{1,0:T(8,128)}), f32[64,1024]{1,0:T(8,128)}) %reduce-scatter.2.cloned.1.call-update) | async-done | bytes 262160 | tf_op jit(solution)/shard_map/reduce_scatter | solution.py:29
  (1 shorter events, 0.0 us)
Async XLA Ops:
  6.5 2.1 copy-start
  6.5 3.1 %copy-start.1 = (f32[1,64,64]{2,1,0:T(8,128)S(1)}, f32[1,64,64]{2,1,0:T(8,128)}, u32[]{:S(2)}) copy-start(f32[1,64,64]{2,1,0:T(8,128)} %param.9) | copy-start | bytes 49156
  6.5 142.9 %all-gather.2.cloned.1.call-start = ((), (), s32[]{:S(2)}) async-start(), calls=%async_computation.1 | async-start | bytes 8912896 | tf_op jit(solution)/shard_map/all_gather | solution.py:23
  9.7 2.5 copy-start.2
  9.7 3.5 %copy-start.3 = (s32[1024]{0:T(1024)S(1)}, s32[1024]{0:T(1024)}, u32[]{:S(2)}) copy-start(s32[1024]{0:T(1024)} %param.11) | copy-start | bytes 12292
  13.2 233.4 %reduce-scatter.2.cloned.1.call-start = ((), (), s32[]{:S(2)}) async-start(), calls=%async_computation.2 | async-start | bytes 4456448 | tf_op jit(solution)/shard_map/reduce_scatter | solution.py:29
Sparse Core Ops, SparseCore 0:
  13.3 136.1 all-gather.1
  178.2 68.3 reduce-scatter.1
where the time goes:
time: 254 us; the launch traced here: 253 us
  waiting for transfers between devices  205 us (81%)
  matrix products  17.9 us (7%)
  between operations  13.5 us (5%)
  local copies, waits for them, and re-layouts  11.3 us (4%)
  other arithmetic  5.89 us (2%)
    all_gather x1, waiting for transfers between devices, per_device(): lax.all_gather(scaled_flat, 'query', axis=0, tiled=True)  136 us
    reduce_scatter x1, waiting for transfers between devices, per_device(): return lax.psum_scatter(ordered, 'layer', scatter_dimension=0, tiled=True)  68.5 us
    dot_general x1, matrix products, per_device(): lax.dot_general(lax.all_gather(scaled_flat, 'query', axis=0, tiled=True),...  15.1 us
    gather x1, local copies, waits for them, and re-layouts, per_device(): ordered = partial_sum[train_order] * factor  8.54 us
  transfers between devices with their start and end apart: 2, of which 2 were waited for; matrix products, arithmetic and copies ran while one was open for 0% of the time, Pallas kernels for 0%

commit v1 on v0

--- a/solution.py
+++ b/solution.py
@@ -20,7 +20,9 @@
     layer_devices = lax.axis_size("layer")
     factor = 1.0 / jnp.sqrt(jnp.float32(local_layers * layer_devices * feat_size))
     partial_sum = lax.dot_general(
-        lax.all_gather(scaled_flat, "query", axis=0, tiled=True),
+        jnp.concatenate(
+            lax.all_to_all(jnp.stack([scaled_flat] * lax.axis_size("query")), "query", 0, 0), axis=0
+        ),
         query_flat,
         (((1,), (1,)), ((), ())),
         preferred_element_type=jnp.float32,

time: 254 us -> 325 us (1.28)
  waiting for transfers between devices: 205 us -> 261 us
  starting transfers between devices: 0.04 us -> 11.6 us
  local copies, waits for them, and re-layouts: 11.3 us -> 15.6 us
    all_to_all x0 -> x1, waiting for transfers between devices: none -> 190 us  [per_device(): lax.all_to_all(jnp.stack([scaled_flat] * lax.axis_size('query')), 'query'...]
    all_gather x1 -> x0, waiting for transfers between devices: 136 us -> none  [per_device(): lax.all_gather(scaled_flat, 'query', axis=0, tiled=True)]
    all_to_all x0 -> x1, starting transfers between devices: none -> 11.6 us  [per_device(): lax.all_to_all(jnp.stack([scaled_flat] * lax.axis_size('query')), 'query'...]
    another operation x0 -> x1, local copies, waits for them, and re-layouts: none -> 4.28 us  [per_device(): jnp.stack([scaled_flat] * lax.axis_size('query'))]
where the time goes in v1:
time: 325 us
  waiting for transfers between devices  261 us (80%)
  matrix products  17.9 us (6%)
  local copies, waits for them, and re-layouts  15.6 us (5%)
  between operations  13.5 us (4%)
  starting transfers between devices  11.6 us (4%)
  other arithmetic  5.06 us (2%)
    all_to_all x1, waiting for transfers between devices, per_device(): lax.all_to_all(jnp.stack([scaled_flat] * lax.axis_size('query')), 'query'...  190 us
    reduce_scatter x1, waiting for transfers between devices, per_device(): return lax.psum_scatter(ordered, 'layer', scatter_dimension=0, tiled=True)  70.7 us
    dot_general x1, matrix products, per_device(): lax.dot_general(jnp.concatenate(lax.all_to_all(jnp.stack([scaled_flat] *...  15.1 us
    all_to_all x1, starting transfers between devices, per_device(): lax.all_to_all(jnp.stack([scaled_flat] * lax.axis_size('query')), 'query'...  11.6 us
    gather x1, local copies, waits for them, and re-layouts, per_device(): ordered = partial_sum[train_order] * factor  8.55 us
  transfers between devices with their start and end apart: 2, of which 2 were waited for; matrix products, arithmetic and copies ran while one was open for 0% of the time, Pallas kernels for 0%

profile of v1, /device:TPU:16, one launch (start us, length us, event | category | flops | bytes accessed | tf_op | source)
XLA Modules:
  0.0 324.6 jit_solution(16178320465056911024)
XLA Ops:
  6.5 0.0 copy-start
  6.5 0.0 copy-start.1
  6.5 2.1 reshape.40
  8.6 0.0 copy-done
  8.6 1.1 fusion.4
  9.7 0.0 copy-done.1
  9.7 0.0 copy-start.2
  9.7 1.8 fusion.2
  11.5 0.7 transpose.5
  12.1 0.0 copy-done.2
  12.2 0.1 divide_convert_fusion
  12.2 4.3 %stack.3 = bf16[16,64,4096]{2,1,0:T(8,128)(2,1)} broadcast(bf16[64,4096]{1,0:T(8,128)(2,1)S(1)} %divide_convert_fusion), dimensions={1,2} | broadcast | bytes 8912896 | tf_op jit(solution)/shard_map/stack | solution.py:24
  16.5 0.0 copy-start.3
  16.5 11.6 %all-to-all-start = ((bf16[16,64,4096]{2,1,0:T(8,128)(2,1)}), bf16[16,64,4096]{2,1,0:T(8,128)(2,1)}, u32[]{:S(2)}, u32[]{:S(2)}) async-start(bf16[16,64,4096]{2,1,0:T(8,128)(2,1)} %stack.3), calls=%async_computation | async-start | bytes 16777216 | tf_op jit(solution)/shard_map/all_to_all | solution.py:24
  28.1 0.0 reduce-scatter.2.cloned.1.call-start
  28.1 0.0 copy-done.3
  28.2 190.2 %all-to-all-done = bf16[16,64,4096]{2,1,0:T(8,128)(2,1)} async-done(((bf16[16,64,4096]{2,1,0:T(8,128)(2,1)}), bf16[16,64,4096]{2,1,0:T(8,128)(2,1)}, u32[]{:S(2)}, u32[]{:S(2)}) %all-to-all-start) | async-done | bytes 8388640 | tf_op jit(solution)/shard_map/all_to_all | solution.py:24
  218.4 15.1 %fusion = f32[1024,1024]{1,0:T(8,128)} fusion(bf16[1024,4096]{1,0:T(8,128)(2,1)} %bitcast.5, bf16[1024,1,4096]{2,0,1:T(8,128)(2,1)} %param.6), kind=kOutput, calls=%fused_computation.1 | convolution fusion | flops 8589934592 | bytes 20971520 | tf_op jit(solution)/shard_map/dot_general | solution.py:22
  233.5 8.6 %gather_fusion = f32[1024,1024]{1,0:T(8,128)} fusion(f32[1024,1024]{1,0:T(8,128)} %fusion, s32[1024]{0:T(1024)S(1)} %fusion.6), kind=kCustom, calls=%fused_computation | custom fusion | bytes 8392704 | tf_op jit(solution)/shard_map/gather | solution.py:30
  242.0 5.0 %broadcast_multiply_fusion = f32[1024,1024]{1,0:T(8,128)} fusion(f32[1024,1024]{1,0:T(8,128)} %gather_fusion), kind=kLoop, calls=%fused_computation.3 | loop fusion | flops 1048576 | bytes 8388608 | tf_op jit(solution)/shard_map/mul | solution.py:30
  247.0 0.0 reduce-scatter.2.cloned.1.call-update
  247.0 70.7 %reduce-scatter.2.cloned.1.call-done = f32[64,1024]{1,0:T(8,128)} async-done(((f32[1024,1024]{1,0:T(8,128)}), f32[64,1024]{1,0:T(8,128)}) %reduce-scatter.2.cloned.1.call-update) | async-done | bytes 262160 | tf_op jit(solution)/shard_map/reduce_scatter | solution.py:31
  (1 shorter events, 0.0 us)
Async XLA Ops:
  6.5 2.1 copy-start
  6.5 3.1 copy-start.1
  9.7 2.5 copy-start.2
  16.5 11.6 %copy-start.3 = (s32[1024]{0:T(1024)S(1)}, s32[1024]{0:T(1024)}, u32[]{:S(2)}) copy-start(s32[1024]{0:T(1024)} %param.11) | copy-start | bytes 12292
  16.5 201.8 %all-to-all-start = ((bf16[16,64,4096]{2,1,0:T(8,128)(2,1)}), bf16[16,64,4096]{2,1,0:T(8,128)(2,1)}, u32[]{:S(2)}, u32[]{:S(2)}) async-start(bf16[16,64,4096]{2,1,0:T(8,128)(2,1)} %stack.3), calls=%async_computation | async-start | bytes 16777216 | tf_op jit(solution)/shard_map/all_to_all | solution.py:24
  28.1 289.6 %reduce-scatter.2.cloned.1.call-start = ((), (), s32[]{:S(2)}) async-start(), calls=%async_computation.2 | async-start | bytes 4456448 | tf_op jit(solution)/shard_map/reduce_scatter | solution.py:31
Sparse Core Ops, SparseCore 0:
  247.1 70.5 reduce-scatter.1
